TPU v7x, 256 devices: a whole 4x4x8 slice. The times are simulated.
256 devices in a mesh: dp: 16 (over z, core), expert: 16 (over x, y).
Axes of the slice: x: 4, y: 4, z: 8, core: 2. Of those that a mesh axis runs over, the one named last changes fastest.
Arguments:
- history: bfloat16 [512, 1024, 2048], P(('dp', 'expert')), may hold values from -6 to 6
- lengths: int32 [512], P(('dp', 'expert')), may hold values from 64 to 1024, as said below
- user_query: bfloat16 [512, 2048], P(('dp', 'expert')), may hold values from -1000 to 1000
- pos_item: bfloat16 [512, 2048], P(('dp', 'expert')), may hold values from -6 to 6
- neg_index: int32 [512, 63], P(('dp', 'expert')), may hold values from 0 to 511
- routes: int32 [32768, 2], P(('dp', 'expert')), may hold values from 0 to 15, all different within a row; in each aligned block of 128 rows (0 to 127, 128 to 255, ...) at most 32 rows name the same one
- w_router: bfloat16 [2048, 16], replicated, may hold values from -0.125 to 0.125
- w_gate: bfloat16 [16, 2048, 768], P('expert', 'dp'), may hold values from -0.125 to 0.125
- w_up: bfloat16 [16, 2048, 768], P('expert', 'dp'), may hold values from -0.125 to 0.125
- w_down: bfloat16 [16, 768, 2048], P('expert', None, 'dp'), may hold values from -0.21875 to 0.21875
- out_gain: float32 [2048], replicated, may hold values from 0.25 to 1.75
Outputs:
- losses: float32 [512], P(('dp', 'expert'))
- grad_gate: float32 [16, 2048, 768], P('expert', 'dp')
- grad_up: float32 [16, 2048, 768], P('expert', 'dp')
- grad_down: float32 [16, 768, 2048], P('expert', None, 'dp')
- grad_router: float32 [2048, 16], replicated
Inputs may be any that keep to these rules, and one draw needn't show every extreme that they name: `lengths`: every device's block of 2 users holds one user with all 1024 events. `neg_index`: indices of users anywhere in the batch. `routes`: each row names two different experts; among the rows of one device no expert is named more than 32 times, a bound that some block reaches.
All inputs are finite; a program needn't handle non-finite values.
Results may differ from a plain program's by a relative error of at most 0.017.
Values may be sent and summed in bfloat16 or wider, within the bound.
A program may use at most 128 MiB of HBM per device.

v0:
```python
import math

import jax
import jax.numpy as jnp
from jax import lax
from jax.sharding import Mesh
from jax.sharding import PartitionSpec as P

D = 2048
HEADS = 16
HEAD = 128
FF = 768
CANDS = 64
EXPERT = ("expert_0", "expert_1")
DP = ("dp_0", "dp_1")
DP_EXPERT = ("dp_0", "dp_1", "expert_0", "expert_1")


norm_eps = 1e-06
loss_scale = 1024.0


def sent_together(arrays, axis, dim, along):
    widths = [a.shape[along] for a in arrays]
    both = jnp.concatenate(arrays, axis=along)
    result = lax.all_gather(both, axis, axis=dim, tiled=True)
    return tuple(jnp.split(result, [sum(widths[:k]) for k in range(1, len(widths))], axis=along))


def whole_of(x, axes, dim):
    result = x
    for number in range(len(axes) - 1, -1, -1):
        result = lax.all_gather(result, axes[number], axis=dim, tiled=True)
    return result


def over_axes_2(x, axes):
    for axis in axes:
        x = lax.psum(x, axis)
    return x


def silu_pair(pre_act):
    sigma_val = jax.nn.sigmoid(pre_act)
    return (pre_act * sigma_val, sigma_val * (1.0 + pre_act * (1.0 - sigma_val)))


def rms_round(values):
    scale_inv = lax.rsqrt(jnp.mean(values * values, axis=-1, keepdims=True) + norm_eps)
    return (values * scale_inv).astype(jnp.bfloat16)


def local(
    history,
    lengths,
    user_query,
    pos_item,
    neg_index,
    routes,
    w_router,
    w_gate,
    w_up,
    w_down,
    out_gain,
):
    user_count = history.shape[0]
    hist_len = history.shape[1]
    model_width = history.shape[2]
    experts = w_router.shape[1]
    expert_devs = lax.axis_size(EXPERT)
    capacity = 4 * user_count * CANDS // experts
    slot_count = expert_devs * capacity
    row_total = user_count * CANDS
    query_heads = user_query.reshape(user_count, HEADS, HEAD)
    key_heads = history.reshape(user_count, hist_len, HEADS, HEAD)
    scores = jnp.einsum(
        "uhd,uthd->uht", query_heads, key_heads, preferred_element_type=jnp.float32
    ) / math.sqrt(HEAD)
    live_mask = jnp.arange(hist_len, dtype=jnp.int32)[None, None, :] < lengths[:, None, None]
    scores = jnp.where(live_mask, scores, -1e30)
    top_val = jnp.max(scores, axis=-1, keepdims=True)
    weights = jnp.where(live_mask, jnp.exp(scores - top_val), 0.0)
    attn_probs = (weights / jnp.sum(weights, axis=-1, keepdims=True)).astype(jnp.bfloat16)
    context = jnp.einsum(
        "uht,uthd->uhd", attn_probs, key_heads, preferred_element_type=jnp.float32
    ).reshape(user_count, model_width)
    all_items = lax.all_gather(pos_item, DP_EXPERT, axis=0, tiled=True)
    candidates = jnp.concatenate([pos_item[:, None, :], all_items[neg_index]], axis=1)
    x_sum = candidates.astype(jnp.float32) + context[:, None, :]
    normed = rms_round(x_sum).reshape(row_total, model_width)
    logits = jnp.dot(normed, w_router, preferred_element_type=jnp.float32)
    affinity = jax.nn.sigmoid(jnp.take_along_axis(logits, routes, axis=1))
    aff_total = jnp.sum(affinity, axis=1, keepdims=True)
    mix = affinity / aff_total
    flat_routes = routes.reshape(-1)
    one_hot = (flat_routes[:, None] == jnp.arange(experts, dtype=jnp.int32)[None, :]).astype(
        jnp.int32
    )
    slot_rank = jnp.sum(jnp.cumsum(one_hot, axis=0) * one_hot, axis=1) - 1
    slot_dest = flat_routes * capacity + slot_rank
    user_base = (lax.axis_index(DP) * expert_devs + lax.axis_index(EXPERT)) * user_count
    own_users = user_base + jnp.arange(user_count, dtype=jnp.int32)
    item_ids = jnp.concatenate([own_users[:, None], neg_index], axis=1).reshape(-1)
    user_ids = (own_users[:, None] + jnp.zeros((user_count, CANDS), jnp.int32)).reshape(-1)
    item_send = (
        jnp.zeros((experts * capacity,), jnp.int32).at[slot_dest].set(jnp.repeat(item_ids, 2))
    )
    user_send = (
        jnp.full((experts * capacity,), -1, jnp.int32).at[slot_dest].set(jnp.repeat(user_ids, 2))
    )
    item_got, user_got = (
        lax.all_to_all(
            item_send.reshape(experts, capacity), EXPERT, split_axis=0, concat_axis=0, tiled=True
        ),
        lax.all_to_all(
            user_send.reshape(experts, capacity), EXPERT, split_axis=0, concat_axis=0, tiled=True
        ),
    )
    group_ctx = lax.all_gather(context, EXPERT, axis=0, tiled=True)
    user_flat = user_got.reshape(-1)
    live_slot = (user_flat >= 0)[:, None]
    local_user = jnp.maximum(user_flat - lax.axis_index(DP) * expert_devs * user_count, 0)
    rebuilt = all_items[item_got.reshape(-1)].astype(jnp.float32) + group_ctx[local_user]
    rows_in = jnp.where(live_slot, rms_round(rebuilt), jnp.zeros((), jnp.bfloat16))
    pieces = sent_together((w_gate[0], w_up[0]), DP, 0, 1)
    columns = rows_in
    gate_pre = jnp.dot(columns, pieces[0], preferred_element_type=jnp.float32)
    up_pre = jnp.dot(columns, pieces[1], preferred_element_type=jnp.float32)
    silu_val, silu_grad = silu_pair(gate_pre)
    hidden = (silu_val * up_pre).astype(jnp.bfloat16)
    expert_out = jnp.dot(
        hidden, whole_of(w_down[0], DP, 1), preferred_element_type=jnp.float32
    ).astype(jnp.bfloat16)
    returned = lax.all_to_all(
        expert_out.reshape(expert_devs, capacity, model_width),
        EXPERT,
        split_axis=0,
        concat_axis=0,
        tiled=True,
    )
    mixed_in = returned.reshape(experts * capacity, model_width)[slot_dest].reshape(
        row_total, 2, model_width
    )
    moe_sum = mix[:, 0:1] * mixed_in[:, 0].astype(jnp.float32) + mix[:, 1:2] * mixed_in[
        :, 1
    ].astype(jnp.float32)
    h_rows = (x_sum.reshape(row_total, model_width) + moe_sum).reshape(
        user_count, CANDS, model_width
    )
    inv_rms = lax.rsqrt(jnp.mean(h_rows * h_rows, axis=-1, keepdims=True) + norm_eps)
    unit_rows = h_rows * inv_rms
    scored = unit_rows * out_gain
    query_f = user_query.astype(jnp.float32)
    listwise = jnp.einsum(
        "ucd,ud->uc", scored, query_f, precision=lax.Precision.HIGHEST
    ) / math.sqrt(D)
    top_list = jnp.max(listwise, axis=-1, keepdims=True)
    expo = jnp.exp(listwise - top_list)
    expo_total = jnp.sum(expo, axis=-1, keepdims=True)
    losses = jnp.log(expo_total[:, 0]) + top_list[:, 0] - listwise[:, 0]
    first_one = (jnp.arange(CANDS, dtype=jnp.int32) == 0).astype(jnp.float32)[None, :]
    d_list = loss_scale * (expo / expo_total - first_one)
    d_scored = d_list[..., None] * query_f[:, None, :] / math.sqrt(D)
    d_unit = d_scored * out_gain
    d_h = inv_rms * (d_unit - unit_rows * jnp.mean(d_unit * unit_rows, axis=-1, keepdims=True))
    d_h = d_h.reshape(row_total, model_width)
    d_out = (mix[:, :, None] * d_h[:, None, :]).astype(jnp.bfloat16)
    d_mix = jnp.sum(d_h[:, None, :] * mixed_in.astype(jnp.float32), axis=-1)
    mix_dot = jnp.sum(mix * d_mix, axis=1, keepdims=True)
    d_aff = (d_mix - mix_dot) / aff_total
    d_pick = d_aff * affinity * (1.0 - affinity)
    route_hot = (routes[:, :, None] == jnp.arange(experts, dtype=jnp.int32)).astype(jnp.float32)
    d_logits = jnp.sum(route_hot * d_pick[:, :, None], axis=1).astype(jnp.bfloat16)
    contract_rows = (((0,), (0,)), ((), ()))
    router_term = lax.dot_general(
        normed, d_logits, contract_rows, preferred_element_type=jnp.float32
    )
    grad_send = (
        jnp.zeros((experts * capacity, model_width), jnp.bfloat16)
        .at[slot_dest]
        .set(d_out.reshape(-1, model_width))
    )
    grad_rows = lax.all_to_all(
        grad_send.reshape(experts, capacity, model_width),
        EXPERT,
        split_axis=0,
        concat_axis=0,
        tiled=True,
    ).reshape(slot_count, model_width)
    contract_cols = (((1,), (1,)), ((), ()))
    columns = grad_rows
    d_hidden = lax.dot_general(
        columns, whole_of(w_down[0], DP, 1), contract_cols, preferred_element_type=jnp.float32
    )
    d_gate = (d_hidden * up_pre * silu_grad).astype(jnp.bfloat16)
    d_up = (d_hidden * silu_val).astype(jnp.bfloat16)
    summed = lax.psum_scatter(
        jnp.concatenate(
            [
                lax.dot_general(rows_in, d_gate, contract_rows, preferred_element_type=jnp.float32),
                lax.dot_general(rows_in, d_up, contract_rows, preferred_element_type=jnp.float32),
                lax.dot_general(
                    grad_rows, hidden, contract_rows, preferred_element_type=jnp.float32
                ),
            ],
            axis=1,
        ).astype(jnp.bfloat16),
        DP,
        scatter_dimension=0,
        tiled=True,
    ).astype(jnp.float32)
    grad_gate = summed[:, :FF][None]
    grad_up = summed[:, FF : 2 * FF][None]
    grad_down = summed[:, 2 * FF :].T[None]
    grad_router = over_axes_2(router_term, DP_EXPERT)
    return (losses, grad_gate, grad_up, grad_down, grad_router)


def solution(mesh):
    torus = Mesh(mesh.devices.reshape(8, 2, 4, 4), ("dp_0", "dp_1", "expert_0", "expert_1"))
    return jax.shard_map(
        local,
        mesh=torus,
        in_specs=(
            P(DP_EXPERT, None, None),
            P(DP_EXPERT),
            P(DP_EXPERT, None),
            P(DP_EXPERT, None),
            P(DP_EXPERT, None),
            P(DP_EXPERT, None),
            P(),
            P(EXPERT, DP, None),
            P(EXPERT, DP, None),
            P(EXPERT, None, DP),
            P(),
        ),
        out_specs=(
            P(DP_EXPERT),
            P(EXPERT, DP, None),
            P(EXPERT, DP, None),
            P(EXPERT, None, DP),
            P(),
        ),
        check_vma=False,
    )
```

profile of v0, /device:TPU:1, one launch (start us, length us, event | category | flops | bytes accessed | tf_op | source)
XLA Modules:
  0.0 580.3 jit_solution(2815404170481698003)
XLA Ops:
  15.3 7.6 %all-to-all-start = ((s32[16,1,32]{2,1,0:T(1,128)}), s32[16,1,32]{2,1,0:T(1,128)S(1)}, u32[]{:S(2)}, u32[]{:S(2)}) async-start(s32[16,1,32]{2,1,0:T(1,128)} %all_to_all.18), calls=%async_computation | async-start | bytes 16384 | tf_op jit(solution)/shard_map/all_to_all | solution.py:115
  22.9 4.5 all-gather
  27.5 5.7 fusion.2
  33.5 5.1 fusion.4
  38.8 19.5 %all-gather.3 = f32[16,2,2048]{2,1,0:T(2,128)S(1)} all-gather(f32[1,2,2048]{2,1,0:T(2,128)S(1)} %reshape.537), channel_id=1, replica_groups=mesh['dp_0'=8,'dp_1'=2,'expert_0'=4,'expert_1'=4] {'expert_0','expert_1'}, dimensions={0}, use_global_device_ids=true | all-gather | bytes 278528 | tf_op jit(solution)/shard_map/all_gather | solution.py:119
  63.5 4.4 all-to-all-start.1
  68.1 6.2 %all-to-all-done.1 = s32[16,1,32]{2,1,0:T(1,128)S(1)} async-done(((s32[16,1,32]{2,1,0:T(1,128)}), s32[16,1,32]{2,1,0:T(1,128)S(1)}, u32[]{:S(2)}, u32[]{:S(2)}) %all-to-all-start.1) | async-done | bytes 2080 | tf_op jit(solution)/shard_map/all_to_all | solution.py:112
  79.3 40.7 %all-gather.12.cloned.1.call-done = bf16[256,2,2048]{2,1,0:T(2,128)(2,1)} async-done(((bf16[1,2,2048]{2,1,0:T(2,128)(2,1)}), bf16[256,2,2048]{2,1,0:T(2,128)(2,1)}) %all-gather.12.cloned.1.call-update) | async-done | bytes 2097168 | tf_op jit(solution)/shard_map/all_gather | solution.py:87
  132.8 34.7 %all-gather.8.cloned.1.call-done = bf16[2048,1536]{1,0:T(8,128)(2,1)} async-done(((bf16[128,1536]{1,0:T(8,128)(2,1)}), bf16[2048,1536]{1,0:T(8,128)(2,1)}) %all-gather.8.cloned.1.call-update) | async-done | bytes 6291472 | tf_op jit(solution)/shard_map/all_gather | solution.py:26
  167.5 4.5 fusion.10
  176.1 43.0 %all-gather.10.cloned.1.call-done = bf16[1,768,2048]{2,1,0:T(8,128)(2,1)} async-done(((bf16[1,768,256]{2,1,0:T(8,128)(2,1)}), bf16[1,768,2048]{2,1,0:T(8,128)(2,1)}) %all-gather.10.cloned.1.call-update) | async-done | bytes 3145744 | tf_op jit(solution)/shard_map/all_gather | solution.py:33
  219.1 5.1 fusion.16
  224.1 6.2 %all-to-all-start.2 = ((bf16[16,32,2048]{2,1,0:T(8,128)(2,1)}), bf16[16,32,2048]{2,1,0:T(8,128)(2,1)}, u32[]{:S(2)}, u32[]{:S(2)}) async-start(bf16[16,32,2048]{2,1,0:T(8,128)(2,1)} %bitcast.109), calls=%async_computation.2 | async-start | bytes 4194304 | tf_op jit(solution)/shard_map/all_to_all | solution.py:134
  235.3 18.1 %all-to-all-done.2 = bf16[16,32,2048]{2,1,0:T(8,128)(2,1)} async-done(((bf16[16,32,2048]{2,1,0:T(8,128)(2,1)}), bf16[16,32,2048]{2,1,0:T(8,128)(2,1)}, u32[]{:S(2)}, u32[]{:S(2)}) %all-to-all-start.2) | async-done | bytes 2097184 | tf_op jit(solution)/shard_map/all_to_all | solution.py:134
  253.4 4.2 gather_fusion.3
  279.9 4.9 scatter_custom_fusion.2
  284.7 8.4 %all-to-all-start.3 = ((bf16[16,32,2048]{2,1,0:T(8,128)(2,1)}), bf16[16,32,2048]{2,1,0:T(8,128)(2,1)}, u32[]{:S(2)}, u32[]{:S(2)}) async-start(bf16[16,32,2048]{2,1,0:T(8,128)(2,1)} %bitcast.108), calls=%async_computation.3 | async-start | bytes 4194304 | tf_op jit(solution)/shard_map/all_to_all | solution.py:183
  295.4 69.7 %all-reduce.5.cloned.1.call-done = f32[2048,16]{0,1:T(8,128)} async-done(((f32[2048,16]{0,1:T(8,128)}), f32[2048,16]{0,1:T(8,128)}) %all-reduce.5.cloned.1.call-update) | async-done | bytes 131088 | tf_op jit(solution)/shard_map/psum | solution.py:39
  365.2 35.4 %all-reduce.7.cloned.1.call-done = f32[2048,16]{0,1:T(8,128)} async-done(((f32[2048,16]{0,1:T(8,128)}), f32[2048,16]{0,1:T(8,128)}) %all-reduce.7.cloned.1.call-update) | async-done | bytes 131088 | tf_op jit(solution)/shard_map/psum | solution.py:39
  412.2 4.4 pad_maximum_fusion
  416.6 12.2 %copy.109 = bf16[2048,2304]{1,0:T(8,128)(2,1)} copy(bf16[2048,2304]{0,1:T(8,128)(2,1)} %pad_maximum_fusion) | data formatting | bytes 18874368
  429.5 18.3 %all-reduce.9.cloned.1.call-done = f32[2048,16]{0,1:T(8,128)} async-done(((f32[2048,16]{0,1:T(8,128)}), f32[2048,16]{0,1:T(8,128)}) %all-reduce.9.cloned.1.call-update) | async-done | bytes 131088 | tf_op jit(solution)/shard_map/psum | solution.py:39
  447.8 74.9 %reduce-scatter.4.cloned.1.call-done = bf16[128,2304]{1,0:T(8,128)(2,1)} async-done(((bf16[2048,2304]{1,0:T(8,128)(2,1)}), bf16[128,2304]{1,0:T(8,128)(2,1)}) %reduce-scatter.4.cloned.1.call-update) | async-done | bytes 589840
  526.8 44.6 %all-reduce.11.cloned.1.call-done = f32[2048,16]{0,1:T(8,128)} async-done(((f32[2048,16]{0,1:T(8,128)}), f32[2048,16]{0,1:T(8,128)}) %all-reduce.11.cloned.1.call-update) | async-done | bytes 131088 | tf_op jit(solution)/shard_map/psum | solution.py:39
  (181 shorter events, 82.9 us)
Async XLA Ops:
  7.2 225.1 %copy-start = (bf16[2048,16]{0,1:T(8,128)(2,1)S(1)}, bf16[2048,16]{0,1:T(8,128)(2,1)}, u32[]{:S(2)}) copy-start(bf16[2048,16]{0,1:T(8,128)(2,1)} %param.17) | copy-start | bytes 196612
  7.2 20.3 %copy-start.16 = (s32[2]{0:T(128)S(1)}, s32[2]{0:T(128)}, u32[]{:S(2)}) copy-start(s32[2]{0:T(128)} %param.12) | copy-start | bytes 28
  7.2 20.3 %copy-start.11 = (bf16[2,2048]{1,0:T(2,128)(2,1)S(1)}, bf16[2,2048]{1,0:T(2,128)(2,1)}, u32[]{:S(2)}) copy-start(bf16[2,2048]{1,0:T(2,128)(2,1)} %param.13) | copy-start | bytes 24580
  7.2 112.8 %all-gather.12.cloned.1.call-start = ((), (), s32[]{:S(2)}) async-start(), calls=%async_computation.11 | async-start | bytes 2105344 | tf_op jit(solution)/shard_map/all_gather | solution.py:87
  7.9 159.6 %all-gather.8.cloned.1.call-start = ((), (), s32[]{:S(2)}) async-start(), calls=%async_computation.5 | async-start | bytes 6684672 | tf_op jit(solution)/shard_map/all_gather | solution.py:26
  15.3 48.2 %all-to-all-start = ((s32[16,1,32]{2,1,0:T(1,128)}), s32[16,1,32]{2,1,0:T(1,128)S(1)}, u32[]{:S(2)}, u32[]{:S(2)}) async-start(s32[16,1,32]{2,1,0:T(1,128)} %all_to_all.18), calls=%async_computation | async-start | bytes 16384 | tf_op jit(solution)/shard_map/all_to_all | solution.py:115
  22.8 196.2 %all-gather.10.cloned.1.call-start = ((), (), s32[]{:S(2)}) async-start(), calls=%async_computation.10 | async-start | bytes 3538944 | tf_op jit(solution)/shard_map/all_gather | solution.py:33
  33.4 5.1 copy-start.15
  33.5 5.3 copy-start.13
  33.5 27.4 %copy-start.12 = (bf16[2,2048]{1,0:T(2,128)(2,1)S(1)}, bf16[2,2048]{1,0:T(2,128)(2,1)}, u32[]{:S(2)}) copy-start(bf16[2,2048]{1,0:T(2,128)(2,1)} %param.14) | copy-start | bytes 24580
  63.5 10.8 %all-to-all-start.1 = ((s32[16,1,32]{2,1,0:T(1,128)}), s32[16,1,32]{2,1,0:T(1,128)S(1)}, u32[]{:S(2)}, u32[]{:S(2)}) async-start(s32[16,1,32]{2,1,0:T(1,128)} %all_to_all.20), calls=%async_computation.1 | async-start | bytes 16384 | tf_op jit(solution)/shard_map/all_to_all | solution.py:112
  126.0 4.7 copy-start.3
  167.5 5.6 copy-start.7
  167.5 5.6 copy-start.17
  176.1 48.0 %copy-start.21 = (bf16[512,768]{1,0:T(8,128)(2,1)}, bf16[512,768]{1,0:T(8,128)(2,1)S(1)}, u32[]{:S(2)}) copy-start(bf16[512,768]{1,0:T(8,128)(2,1)S(1)} %get-tuple-element.59) | copy-start | bytes 2359300
  224.1 6.2 %copy-start.14 = (f32[2048]{0:T(1024)S(1)}, f32[2048]{0:T(1024)}, u32[]{:S(2)}) copy-start(f32[2048]{0:T(1024)} %param.21) | copy-start | bytes 24580
  224.1 29.3 %all-to-all-start.2 = ((bf16[16,32,2048]{2,1,0:T(8,128)(2,1)}), bf16[16,32,2048]{2,1,0:T(8,128)(2,1)}, u32[]{:S(2)}, u32[]{:S(2)}) async-start(bf16[16,32,2048]{2,1,0:T(8,128)(2,1)} %bitcast.109), calls=%async_computation.2 | async-start | bytes 4194304 | tf_op jit(solution)/shard_map/all_to_all | solution.py:134
  284.7 116.1 %all-to-all-start.3 = ((bf16[16,32,2048]{2,1,0:T(8,128)(2,1)}), bf16[16,32,2048]{2,1,0:T(8,128)(2,1)}, u32[]{:S(2)}, u32[]{:S(2)}) async-start(bf16[16,32,2048]{2,1,0:T(8,128)(2,1)} %bitcast.108), calls=%async_computation.3 | async-start | bytes 4194304 | tf_op jit(solution)/shard_map/all_to_all | solution.py:183
  293.2 72.0 %all-reduce.5.cloned.1.call-start = ((), (), s32[]{:S(2)}) async-start(), calls=%async_computation.6 | async-start | bytes 262144 | tf_op jit(solution)/shard_map/psum | solution.py:39
  295.4 105.3 %all-reduce.7.cloned.1.call-start = ((), (), s32[]{:S(2)}) async-start(), calls=%async_computation.7 | async-start | bytes 262144 | tf_op jit(solution)/shard_map/psum | solution.py:39
  365.2 82.6 %all-reduce.9.cloned.1.call-start = ((), (), s32[]{:S(2)}) async-start(), calls=%async_computation.8 | async-start | bytes 262144 | tf_op jit(solution)/shard_map/psum | solution.py:39
  400.7 122.0 %reduce-scatter.4.cloned.1.call-start = ((), (), s32[]{:S(2)}) async-start(), calls=%async_computation.12 | async-start | bytes 10027008
  428.8 142.6 %all-reduce.11.cloned.1.call-start = ((), (), s32[]{:S(2)}) async-start(), calls=%async_computation.9 | async-start | bytes 262144 | tf_op jit(solution)/shard_map/psum | solution.py:39
  524.1 48.9 %copy-start.1 = (bf16[2048,16]{0,1:T(8,128)(2,1)S(1)}, bf16[2048,16]{0,1:T(8,128)(2,1)}, u32[]{:S(2)}) copy-start(bf16[2048,16]{0,1:T(8,128)(2,1)} %param.17) | copy-start | bytes 196612
  (11 other events, 29.0 us)
Sparse Core Ops, SparseCore 0:
  11.8 108.1 all-gather.11
  122.4 45.0 all-gather.7
  169.2 49.7 all-gather.9
  296.6 68.5 all-reduce.4
  367.8 32.8 all-reduce.6
  403.0 44.7 all-reduce.8
  450.3 72.3 reduce-scatter.3
  525.0 46.3 all-reduce.10
where the time goes:
time: 590 us; the launch traced here: 580 us
  waiting for transfers between devices  386 us (65%)
  local copies, waits for them, and re-layouts  59.2 us (10%)
  matrix products  36.6 us (6%)
  other arithmetic  31.9 us (5%)
  starting transfers between devices  26.9 us (5%)
  blocking collectives  24 us (4%)
  between operations  15.2 us (3%)
    psum x4, waiting for transfers between devices, over_axes_2(): x = lax.psum(x, axis)  168 us
    unnamed x9, waiting for transfers between devices  75.7 us
    all_gather x1, waiting for transfers between devices, whole_of(): result = lax.all_gather(result, axes[number], axis=dim, tiled=True)  43 us
    all_gather x1, waiting for transfers between devices, local(): all_items = lax.all_gather(pos_item, DP_EXPERT, axis=0, tiled=True)  40.7 us
    all_gather x1, waiting for transfers between devices, sent_together(): result = lax.all_gather(both, axis, axis=dim, tiled=True)  34.7 us
    unnamed x59, local copies, waits for them, and re-layouts  26.9 us
    all_gather x1, blocking collectives, local(): group_ctx = lax.all_gather(context, EXPERT, axis=0, tiled=True)  19.5 us
    all_to_all x1, waiting for transfers between devices, local(): lax.all_to_all(expert_out.reshape(expert_devs, capacity, model_width), EX...  18.1 us
  transfers between devices with their start and end apart: 12, of which 10 were waited for; matrix products, arithmetic and copies ran while one was open for 15% of the time, Pallas kernels for 0%

commit v1 on v0

v1 whole, which is shorter than its diff:
```python
import functools
import math

import jax
import jax.numpy as jnp
from jax import lax
from jax.experimental import pallas as pl
from jax.experimental.pallas import tpu as pltpu
from jax.sharding import PartitionSpec as P

HEAD = 128
CANDS = 64
EPS = 1e-6
LOSS_SCALE = 1024.0
LANES = 128

f32, bf16, i32 = jnp.float32, jnp.bfloat16, jnp.int32
NT = (((1,), (1,)), ((), ()))
TN = (((0,), (0,)), ((), ()))


def dot(a, b):
    return jnp.dot(a, b, preferred_element_type=f32)


def iota(shape, dim):
    return lax.broadcasted_iota(i32, shape, dim)


def kernel(
    sizes,
    hist, lens, q_ref, pos_ref, lane_ints, col_ints, wr_ref, wg, wu, wd, gain_ref,
    loss_out, gg_out, gu_out, gd_out, gr_out,
    bufs, w_g, w_u, w_d, tab, pieces, ctx_pieces, ctx2, codes_out, codes,
    s01, st, xh, nloc, gq_ref, xbuf, rows, rows_t, acc_g, acc_u, acc_h,
    hid, hid_t, d_gu, r_part, r_got, r_mid, r_fin,
    g_own, g_out, g_sib, d_own, d_out, d_sib, g_ring, d_ring,
    hist_sem, own_sem, small_s, small_r, ring_s, ring_r, sib_s, sib_r,
    a_s, a_r, gsib_s, gsib_r, dsib_s, dsib_r, sum_s, sum_r,
):
    Z, E, D, FF, CAP, R = (sizes[k] for k in ("Z", "E", "D", "FF", "CAP", "R"))
    S = E * CAP
    HEADS = D // HEAD
    PC = LANES
    NP = D // PC
    PR = 2 * NP
    FH = FF // 2
    N_ITEMS = 2 * E * 2 * Z
    HALF = N_ITEMS // 2
    BLK = 2 * Z
    TABW = tab.shape[0]
    CH = 2 * LANES

    dp = lax.axis_index("dp")
    me = lax.axis_index("expert")
    z = lax.div(dp, 2)
    c = lax.rem(dp, 2)
    sib_dp = 2 * z + 1 - c

    def at_z(off):
        return lax.rem(z + (off + Z), Z)

    def peer(j):
        if E == 16:
            x, y = lax.div(me, 4), lax.rem(me, 4)
            return lax.rem(x + lax.div(j, 4), 4) * 4 + lax.rem(y + lax.rem(j, 4), 4)
        return lax.rem(me + j, E)

    def mo(v, n):
        return pl.multiple_of(v, n)

    def remote(src, dst, s_sem, r_sem, to_dp, to_e):
        return pltpu.make_async_remote_copy(
            src_ref=src, dst_ref=dst, send_sem=s_sem, recv_sem=r_sem,
            device_id={"dp": to_dp, "expert": to_e},
            device_id_type=pl.DeviceIdType.MESH,
        )

    def took(ref, sem):
        pltpu.make_async_copy(ref, ref, sem).wait()

    def to_peers(make):
        @pl.loop(1, E)
        def _(j):
            make(peer(j)).start()

    drains = []

    hist_copies = [
        pltpu.make_async_copy(hist.at[n // 2, pl.ds((n % 2) * S, S), :], bufs.at[n], hist_sem.at[n])
        for n in range(4)
    ]
    for cp in hist_copies:
        cp.start()

    own = (wg.at[0], wu.at[0], wd.at[0, pl.ds(0, FH), :], wd.at[0, pl.ds(FH, FH), :])

    def wref(t, of):
        if t < 2:
            return (w_g, w_u)[t].at[pl.ds(mo(of * LANES, LANES), LANES), :]
        return w_d.at[pl.ds((t - 2) * FH, FH), pl.ds(mo(of * LANES, LANES), LANES)]

    own_copies = [pltpu.make_async_copy(own[t], wref(t, dp), own_sem.at[t]) for t in range(4)]
    for cp in own_copies:
        cp.start()

    pos = pos_ref[...].astype(f32)
    for u in range(2):
        for j in range(NP):
            pieces[pl.ds(z * PR + NP * u + j, 1), :] = pos[u : u + 1, j * PC : (j + 1) * PC]

    barrier = pltpu.get_barrier_semaphore()

    @pl.loop(1, E)
    def _(j):
        pl.semaphore_signal(
            barrier, inc=1, device_id={"dp": dp, "expert": peer(j)},
            device_id_type=pl.DeviceIdType.MESH,
        )

    @pl.loop(1, 2 * Z)
    def _(j):
        pl.semaphore_signal(
            barrier, inc=1, device_id={"dp": lax.rem(dp + j, 2 * Z), "expert": me},
            device_id_type=pl.DeviceIdType.MESH,
        )

    pl.semaphore_wait(barrier, E - 1 + 2 * Z - 1)

    HOPS = [(Z // 2, Z // 2 - 1), (Z // 2 - 1, Z // 2)] * 2

    def ring_send(t, d, k, src, dst):
        cp = remote(
            src, dst, ring_s.at[t, d, k], ring_r.at[t, d, k],
            2 * at_z(1 if d == 0 else -1) + c, me,
        )
        cp.start()
        drains.append(cp.wait_send)

    def sib_send(t, idx, src, dst):
        cp = remote(src, dst, sib_s.at[t, idx], sib_r.at[t, idx], sib_dp, me)
        cp.start()
        drains.append(cp.wait_send)

    def ring_begin(types):
        for t in types:
            for d in range(2):
                if HOPS[t][d] > 0:
                    ring_send(t, d, 0, own[t], wref(t, dp))
        for t in types:
            sib_send(t, 0, own[t], wref(t, dp))

    def ring_event(types, k):
        for t in types:
            for d in range(2):
                if k > HOPS[t][d]:
                    continue
                off = -k if d == 0 else k
                r = wref(t, 2 * at_z(off) + c)
                took(r, ring_r.at[t, d, k - 1])
                if k < HOPS[t][d]:
                    ring_send(t, d, k, r, r)
                sib_send(t, off % Z, r, r)

    def sib_wait(types, off):
        for t in types:
            took(wref(t, 2 * at_z(off) + 1 - c), sib_r.at[t, off % Z])

    my_piece = pieces.at[pl.ds(mo(z * PR, PR), PR), :]

    @pl.loop(1, Z)
    def _(k):
        remote(
            my_piece, my_piece, small_s.at[0], small_r.at[0],
            2 * lax.rem(z + k, Z) + c, me,
        ).start()

    drains.append(lambda: took(pieces.at[pl.ds(0, (Z - 1) * PR), :], small_s.at[0]))
    ring_begin((0, 1))

    rt0, rt1 = lane_ints[0:1, :], lane_ints[1:2, :]
    id_lane = lane_ints[2:3, :]

    def table_row(i):
        dev = lax.shift_right_logical(i, 1)
        of = lax.div(dev, E)
        return (
            lax.rem(of, 2) * HALF + lax.rem(dev, E) * BLK + lax.div(of, 2) * 2 + (i & 1)
        )

    e_sub = iota((E, R), 0)
    mt0, mt1 = e_sub == rt0, e_sub == rt1
    upper = (iota((R, R), 0) < iota((R, R), 1)).astype(bf16)
    rank_t = dot((mt0 | mt1).astype(bf16), upper) + (CAP * e_sub).astype(f32)
    slot0 = jnp.sum(jnp.where(mt0, rank_t, 0.0), axis=0, keepdims=True).astype(i32)
    slot1 = jnp.sum(jnp.where(mt1, rank_t, 0.0), axis=0, keepdims=True).astype(i32)
    s_sub = iota((S, R), 0)
    in0, in1 = s_sub == slot0, s_sub == slot1
    s01[:, 0:R] = in0.astype(bf16)
    s01[:, R : 2 * R] = in1.astype(bf16)
    user_lane = me * 2 + (iota((1, R), 1) >= CANDS).astype(i32)
    code_lane = (table_row(id_lane) + user_lane * N_ITEMS + 1).astype(f32)
    code = jnp.sum(jnp.where(in0 | in1, code_lane, 0.0), axis=1, keepdims=True).astype(i32) - 1
    codes_out[...] = jnp.broadcast_to(code, (S, LANES))
    my_slots = pl.ds(mo(me * CAP, CAP), CAP)
    codes[my_slots, :] = codes_out[my_slots, :]
    to_peers(
        lambda p: remote(
            codes_out.at[pl.ds(mo(p * CAP, CAP), CAP), :], codes.at[my_slots, :],
            small_s.at[1], small_r.at[1], dp, p,
        )
    )
    drains.append(lambda: took(codes_out.at[pl.ds(0, S - CAP), :], small_s.at[1]))

    r0, r1, id_col = col_ints[:, 0:1], col_ints[:, 1:2], col_ints[:, 2:3]
    e_lane = iota((R, E), 1)
    m0, m1 = e_lane == r0, e_lane == r1
    lower = (iota((R, R), 1) < iota((R, R), 0)).astype(bf16)
    rank = dot(lower, (m0 | m1).astype(bf16)) + (CAP * e_lane).astype(f32)
    s_lane = iota((R, S), 1)
    for k, m in enumerate((m0, m1)):
        slot = jnp.sum(jnp.where(m, rank, 0.0), axis=1, keepdims=True).astype(i32)
        st[k * R : (k + 1) * R, :] = (s_lane == slot).astype(bf16)

    took(pieces.at[pl.ds(0, (Z - 1) * PR), :], small_r.at[0])
    my_block = pl.ds(mo(c * HALF + me * BLK, BLK), BLK)
    for j in range(NP):
        tab[my_block, j * PC : (j + 1) * PC] = pieces[pl.ds(j, BLK, stride=NP), :].astype(bf16)
    to_peers(
        lambda p: remote(
            tab.at[my_block, :], tab.at[my_block, :], small_s.at[2], small_r.at[2], dp, p
        )
    )
    drains.append(lambda: took(tab.at[pl.ds(0, (E - 1) * BLK), :], small_s.at[2]))

    in_head = lax.shift_right_logical(iota((HEADS, D), 1), 7) == iota((HEADS, D), 0)

    def attend(u):
        hist_copies[2 * u].wait()
        hist_copies[2 * u + 1].wait()
        qd = jnp.where(in_head, q_ref[u : u + 1, :].astype(f32), 0.0).astype(bf16)
        halves, tops = [], []
        for n in range(2):
            s = lax.dot_general(qd, bufs[2 * u + n], NT, preferred_element_type=f32)
            s = s * (1.0 / math.sqrt(HEAD))
            live = (iota((HEADS, S), 1) + n * S) < lens[u]
            s = jnp.where(live, s, -1e30)
            halves.append((s, live))
            tops.append(jnp.max(s, axis=1, keepdims=True))
        top = jnp.maximum(tops[0], tops[1])
        w = [jnp.where(live, jnp.exp(s - top), 0.0) for s, live in halves]
        total = jnp.sum(w[0], axis=1, keepdims=True) + jnp.sum(w[1], axis=1, keepdims=True)
        pooled = dot((w[0] / total).astype(bf16), bufs[2 * u]) + dot(
            (w[1] / total).astype(bf16), bufs[2 * u + 1]
        )
        ctx = jnp.sum(jnp.where(in_head, pooled, 0.0), axis=0, keepdims=True)
        ctx2[u : u + 1, :] = ctx
        for j in range(NP):
            ctx_pieces[pl.ds(me * PR + NP * u + j, 1), :] = ctx[:, j * PC : (j + 1) * PC]

    attend(0)
    ring_event((0, 1), 1)
    attend(1)
    my_ctx = ctx_pieces.at[pl.ds(mo(me * PR, PR), PR), :]
    to_peers(lambda p: remote(my_ctx, my_ctx, small_s.at[3], small_r.at[3], dp, p))
    drains.append(lambda: took(ctx_pieces.at[pl.ds(0, (E - 1) * PR), :], small_s.at[3]))

    took(tab.at[pl.ds(0, (E - 1) * BLK), :], small_r.at[2])
    my_half = tab.at[pl.ds(mo(c * HALF, HALF), HALF), :]
    half_copy = remote(my_half, my_half, small_s.at[4], small_r.at[4], sib_dp, me)
    half_copy.start()
    drains.append(half_copy.wait_send)
    for u in range(2):
        gq_ref[u : u + 1, :] = q_ref[u : u + 1, :].astype(f32) * gain_ref[...]
    ring_event((0, 1), 2)
    took(my_half, small_r.at[4])

    first_user = iota((R, 1), 0) < CANDS

    def by_user(ref, cols):
        return jnp.where(first_user, ref[0:1, cols], ref[1:2, cols])

    oh = (iota((R, N_ITEMS), 1) == table_row(id_col)).astype(bf16)
    NC = min(512, D)
    total = jnp.zeros((R, 1), f32)
    for n in range(D // NC):
        cols = slice(n * NC, (n + 1) * NC)
        x = dot(oh, tab[0:N_ITEMS, cols]) + by_user(ctx2, cols)
        xh[:, cols] = x
        total = total + jnp.sum(x * x, axis=1, keepdims=True)
    inv = lax.rsqrt(total * (1.0 / D) + EPS)
    for n in range(D // NC):
        cols = slice(n * NC, (n + 1) * NC)
        nloc[:, cols] = (xh[:, cols] * inv).astype(bf16)
    logits = lax.dot_general(nloc[...], wr_ref[...], NT, preferred_element_type=f32)
    affinity = jax.nn.sigmoid(logits)
    aff0 = jnp.sum(jnp.where(m0, affinity, 0.0), axis=1, keepdims=True)
    aff1 = jnp.sum(jnp.where(m1, affinity, 0.0), axis=1, keepdims=True)
    aff_total = aff0 + aff1
    mix0, mix1 = aff0 / aff_total, aff1 / aff_total

    took(ctx_pieces.at[pl.ds(0, (E - 1) * PR), :], small_r.at[3])
    NU = 2 * E
    for j in range(NP):
        cols = slice(j * PC, (j + 1) * PC)
        v = ctx_pieces[pl.ds(j, NU, stride=NP), :]
        for n in range(3):
            part = v.astype(bf16)
            tab[N_ITEMS + n * NU : N_ITEMS + (n + 1) * NU, cols] = part
            v = v - part.astype(f32)
    tab[N_ITEMS + 3 * NU :, :] = jnp.zeros((TABW - N_ITEMS - 3 * NU, D), bf16)
    took(codes.at[pl.ds(0, S - CAP), :], small_r.at[1])
    ring_event((0, 1), 3) if Z > 6 else None
    MT = min(128, S)

    @pl.loop(0, S // MT)
    def _(m):
        here = pl.ds(mo(m * MT, MT), MT)
        got = codes[here, :]
        item = jnp.where(got >= 0, got & (N_ITEMS - 1), -1)
        user = lax.shift_right_arithmetic(got, N_ITEMS.bit_length() - 1)
        lane = iota((MT, LANES), 1)
        parts = [(item == lane + LANES * b).astype(bf16) for b in range(max(1, N_ITEMS // LANES))]
        if N_ITEMS < LANES:
            parts = [p[:, :N_ITEMS] for p in parts]
        parts.append(((user == lax.rem(lane, NU)) & (lane < 3 * NU)).astype(bf16))
        hot = jnp.concatenate(parts, axis=1)
        ss = jnp.zeros((MT, 1), f32)
        for n in range(D // NC):
            cols = slice(n * NC, (n + 1) * NC)
            x = dot(hot, tab[:, cols])
            xbuf[:, cols] = x
            ss = ss + jnp.sum(x * x, axis=1, keepdims=True)
        scale = lax.rsqrt(ss * (1.0 / D) + EPS)
        for n in range(D // NC):
            cols = slice(n * NC, (n + 1) * NC)
            y = (xbuf[:, cols] * scale).astype(bf16)
            rows[here, cols] = y
            rows_t[cols, here] = y.T

    for k in range(3, Z // 2 + 1) if Z <= 6 else range(4, Z // 2 + 1):
        ring_event((0, 1), k)
    ring_begin((2, 3))

    near_first = [0]
    for k in range(1, Z // 2):
        near_first += [k, -k]
    near_first.append(Z // 2)
    FT = 256

    for off in near_first:
        if off == 0:
            own_copies[0].wait()
            own_copies[1].wait()
        sib_wait((0, 1), off)
        cols = pl.ds(mo(at_z(off) * CH, CH), CH)

        @pl.loop(0, FF // FT)
        def _(n):
            f = pl.ds(mo(n * FT, FT), FT)
            left = rows[:, cols]
            for acc, w in ((acc_g, w_g), (acc_u, w_u)):
                v = dot(left, w[cols, f])
                if off == 0:
                    acc[:, f] = v
                else:
                    acc[:, f] += v

    @pl.loop(0, S // 64)
    def _(m):
        here = pl.ds(mo(m * 64, 64), 64)
        g, up = acc_g[here, :], acc_u[here, :]
        sig = jax.nn.sigmoid(g)
        silu = g * sig
        hid[here, :] = (silu * up).astype(bf16)
        acc_g[here, :] = up * (sig * (1.0 + g * (1.0 - sig)))
        acc_u[here, :] = silu

    def exchange(way, i, cols, src, dst):
        to_peers(
            lambda p: remote(
                bufs.at[src, pl.ds(mo(p * CAP, CAP), CAP), cols], bufs.at[dst, my_slots, cols],
                a_s.at[way, i], a_r.at[way, i], dp, p,
            )
        )
        drains.append(lambda: took(bufs.at[src, pl.ds(0, S - CAP), cols], a_s.at[way, i]))

    done_k = 0
    for i, off in enumerate(near_first):
        if off == 0:
            own_copies[2].wait()
            own_copies[3].wait()
        if abs(off) > done_k:
            done_k = abs(off)
            ring_event((2, 3), done_k)
        sib_wait((2, 3), off)
        cols = pl.ds(mo(at_z(off) * CH, CH), CH)
        bufs[0, :, cols] = dot(hid[...], w_d[:, cols]).astype(bf16)
        bufs[1, my_slots, cols] = bufs[0, my_slots, cols]
        exchange(0, i, cols, 0, 1)

    for n in range(FF // LANES):
        f = slice(n * LANES, (n + 1) * LANES)
        hid_t[f, :] = hid[:, f].T

    sums = [jnp.zeros((R, 1), f32) for _ in range(6)]
    for i, off in enumerate(near_first):
        cols = pl.ds(mo(at_z(off) * CH, CH), CH)
        took(bufs.at[1, pl.ds(0, S - CAP), cols], a_r.at[0, i])
        e = dot(st[...], bufs[1, :, cols])
        e0, e1 = e[0:R], e[R : 2 * R]
        h = xh[:, cols] + mix0 * e0 + mix1 * e1
        xh[:, cols] = h
        gq = by_user(gq_ref, cols)
        terms = (h * h, h * gq, gq * e0, gq * e1, h * e0, h * e1)
        sums = [a + jnp.sum(t, axis=1, keepdims=True) for a, t in zip(sums, terms)]
    hh, hq, qe0, qe1, he0, he1 = sums

    inv_h = lax.rsqrt(hh * (1.0 / D) + EPS)
    listwise = hq * inv_h * (1.0 / math.sqrt(D))
    d_parts = []
    for u in range(2):
        lw = listwise[u * CANDS : (u + 1) * CANDS]
        top = jnp.max(lw, axis=0, keepdims=True)
        ex = jnp.exp(lw - top)
        ex_total = jnp.sum(ex, axis=0, keepdims=True)
        loss = jnp.log(ex_total) + top - lw[0:1]
        loss_out[u : u + 1, :] = jnp.broadcast_to(loss, (1, LANES))
        first = (iota((CANDS, 1), 0) == 0).astype(f32)
        d_parts.append(LOSS_SCALE * (ex / ex_total - first))
    d_list = jnp.concatenate(d_parts, axis=0) * (1.0 / math.sqrt(D))
    alpha = inv_h * d_list
    beta = alpha * inv_h * inv_h * hq * (1.0 / D)

    far_first = near_first[::-1]
    for i, off in enumerate(far_first):
        cols = pl.ds(mo(at_z(off) * CH, CH), CH)
        dh = alpha * by_user(gq_ref, cols) - beta * xh[:, cols]
        both = jnp.concatenate([(mix0 * dh).astype(bf16), (mix1 * dh).astype(bf16)], axis=0)
        bufs[2, :, cols] = dot(s01[...], both).astype(bf16)
        bufs[3, my_slots, cols] = bufs[2, my_slots, cols]
        exchange(1, i, cols, 2, 3)

    d_mix0, d_mix1 = alpha * qe0 - beta * he0, alpha * qe1 - beta * he1
    mix_dot = mix0 * d_mix0 + mix1 * d_mix1
    pick0 = (d_mix0 - mix_dot) / aff_total * aff0 * (1.0 - aff0)
    pick1 = (d_mix1 - mix_dot) / aff_total * aff1 * (1.0 - aff1)
    d_logits = (jnp.where(m0, pick0, 0.0) + jnp.where(m1, pick1, 0.0)).astype(bf16)
    DB = D // E
    r_part[...] = lax.dot_general(d_logits, nloc[...], TN, preferred_element_type=f32)
    my_cols = pl.ds(mo(me * DB, DB), DB)
    r_got[me] = r_part[:, my_cols]
    to_peers(
        lambda p: remote(
            r_part.at[:, pl.ds(mo(p * DB, DB), DB)], r_got.at[me],
            small_s.at[5], small_r.at[5], dp, p,
        )
    )
    drains.append(lambda: took(r_got.at[pl.ds(0, E - 1)], small_s.at[5]))

    def ring_slot(t, d, k):
        return g_ring.at[t, d, k] if t < 2 else d_ring.at[t - 2, d, k]

    def block(three, t, of):
        if t < 2:
            return three[0].at[t, pl.ds(mo(of * LANES, LANES), LANES), :]
        return three[1].at[of, pl.ds((t - 2) * FH, FH), :]

    mine = (g_own, d_own)
    theirs = (g_sib, d_sib)

    def add_rows(t, of, extra, out):
        height = LANES if t < 2 else FH
        step = 64

        @pl.loop(0, height // step)
        def _(m):
            here = pl.ds(mo(m * step, step), step)
            a, b = block(mine, t, of), block(theirs, t, of)
            v = a[here, :].astype(f32) + b[here, :].astype(f32)
            for r in extra:
                v = v + r[here, :].astype(f32)
            if out is None:
                a[here, :] = v.astype(bf16)
            else:
                out[here, :] = v

    def sum_send(t, d, k):
        of = at_z(k if d == 0 else -k)
        extra = []
        if k < HOPS[t][d]:
            r = ring_slot(t, d, k)
            took(r, sum_r.at[t, d, k])
            extra.append(r)
        add_rows(t, of, extra, None)
        cp = remote(
            block(mine, t, of), ring_slot(t, d, k - 1), sum_s.at[t, d, k - 1],
            sum_r.at[t, d, k - 1], 2 * at_z(1 if d == 0 else -1) + c, me,
        )
        cp.start()
        drains.append(cp.wait_send)

    def sum_step(types, k):
        for t in types:
            for d in range(2):
                if k <= HOPS[t][d]:
                    sum_send(t, d, k)

    def sum_last(t, out):
        extra = []
        for d in range(2):
            if HOPS[t][d] > 0:
                r = ring_slot(t, d, 0)
                took(r, sum_r.at[t, d, 0])
                extra.append(r)
        add_rows(t, z, extra, out)

    def down_wait(off):
        took(d_sib.at[at_z(off)], dsib_r.at[off % Z])

    def gate_wait(off):
        for t in range(2):
            took(block(theirs, t, at_z(off)), gsib_r.at[t, off % Z])

    def offs_at(k):
        if k == 0 or k == Z // 2:
            return [k]
        return [k, -k]

    i = 0
    for k in range(Z // 2, -1, -1):
        for off in reversed(offs_at(k)):
            of = at_z(off)
            cols = pl.ds(mo(of * CH, CH), CH)
            took(bufs.at[3, pl.ds(0, S - CAP), cols], a_r.at[1, i])
            got = bufs[3, :, cols]
            v = lax.dot_general(got, w_d[:, cols], NT, preferred_element_type=f32)
            if i == 0:
                acc_h[...] = v
            else:
                acc_h[...] += v
            g = dot(hid_t[...], got)
            low, high = g[:, :LANES], g[:, LANES:]
            d_own[of] = jnp.where(c == 0, low, high).astype(bf16)
            d_out[of] = jnp.where(c == 0, high, low).astype(bf16)
            cp = remote(d_out.at[of], d_sib.at[of], dsib_s.at[off % Z], dsib_r.at[off % Z], sib_dp, me)
            cp.start()
            drains.append(cp.wait_send)
            i += 1
        if k + 1 <= Z // 2:
            for off in offs_at(k + 1):
                down_wait(off)
            sum_step((2, 3), k + 1)

    @pl.loop(0, S // 64)
    def _(m):
        here = pl.ds(mo(m * 64, 64), 64)
        dh = acc_h[here, :]
        d_gu[0, here, :] = (dh * acc_g[here, :]).astype(bf16)
        d_gu[1, here, :] = (dh * acc_u[here, :]).astype(bf16)

    took(r_got.at[pl.ds(0, E - 1)], small_r.at[5])
    part = r_got[0]
    for n in range(1, E):
        part = part + r_got[n]
    r_mid[dp] = part

    @pl.loop(1, 2 * Z)
    def _(j):
        remote(
            r_mid.at[dp], r_mid.at[dp], small_s.at[6], small_r.at[6],
            lax.rem(dp + j, 2 * Z), me,
        ).start()

    drains.append(lambda: took(r_mid.at[pl.ds(0, 2 * Z - 1)], small_s.at[6]))

    for k in range(Z // 2, -1, -1):
        for off in reversed(offs_at(k)):
            of = at_z(off)
            for core, dest in ((c, g_own), (1 - c, g_out)):
                at = pl.ds(mo((2 * of + core) * LANES, LANES), LANES)
                to = pl.ds(mo(of * LANES, LANES), LANES)
                left = rows_t[at, :]
                for t in range(2):
                    dest[t, to, :] = dot(left, d_gu[t]).astype(bf16)
            for t in range(2):
                cp = remote(
                    block((g_out, d_out), t, of), block(theirs, t, of),
                    gsib_s.at[t, off % Z], gsib_r.at[t, off % Z], sib_dp, me,
                )
                cp.start()
                drains.append(cp.wait_send)
        if k + 1 <= Z // 2:
            for off in offs_at(k + 1):
                gate_wait(off)
            sum_step((0, 1), k + 1)

    down_wait(0)
    sum_last(2, gd_out.at[pl.ds(0, FH), :])
    sum_last(3, gd_out.at[pl.ds(FH, FH), :])

    took(r_mid.at[pl.ds(0, 2 * Z - 1)], small_r.at[6])
    part = r_mid[0]
    for n in range(1, 2 * Z):
        part = part + r_mid[n]
    r_fin[me] = part
    to_peers(
        lambda p: remote(r_fin.at[me], r_fin.at[me], small_s.at[7], small_r.at[7], dp, p)
    )
    drains.append(lambda: took(r_fin.at[pl.ds(0, E - 1)], small_s.at[7]))
    took(r_fin.at[pl.ds(0, E - 1)], small_r.at[7])
    for n in range(E):
        gr_out[:, n * DB : (n + 1) * DB] = r_fin[n]

    gate_wait(0)
    sum_last(0, gg_out)
    sum_last(1, gu_out)
    for drain in drains:
        drain()


def local(
    sizes, history, lengths, user_query, pos_item, neg_index, routes,
    w_router, w_gate, w_up, w_down, out_gain,
):
    Z, E, D, FF, CAP, R = (sizes[k] for k in ("Z", "E", "D", "FF", "CAP", "R"))
    S = E * CAP
    base = (lax.axis_index("dp") * E + lax.axis_index("expert")) * 2
    ids = jnp.concatenate(
        [base + jnp.arange(2, dtype=i32)[:, None], neg_index], axis=1
    ).reshape(R)
    lane_ints = jnp.concatenate([routes.T, ids[None, :]], axis=0)
    col_ints = jnp.concatenate([routes, ids[:, None]], axis=1)
    n_items = 4 * Z * E
    tab_rows = n_items + LANES
    H = max(Z // 2, 1)
    dma = pltpu.SemaphoreType.DMA
    vmem = pl.BlockSpec(memory_space=pltpu.VMEM)
    hbm = pl.BlockSpec(memory_space=pl.ANY)
    outs = pl.pallas_call(
        functools.partial(kernel, sizes),
        out_shape=(
            jax.ShapeDtypeStruct((8, LANES), f32),
            jax.ShapeDtypeStruct((LANES, FF), f32),
            jax.ShapeDtypeStruct((LANES, FF), f32),
            jax.ShapeDtypeStruct((FF, LANES), f32),
            jax.ShapeDtypeStruct((E, D), f32),
        ),
        in_specs=[
            hbm, pl.BlockSpec(memory_space=pltpu.SMEM), vmem, vmem, vmem, vmem, vmem,
            hbm, hbm, hbm, vmem,
        ],
        out_specs=(vmem,) * 5,
        scratch_shapes=[
            pltpu.VMEM((4, S, D), bf16),
            pltpu.VMEM((D, FF), bf16),
            pltpu.VMEM((D, FF), bf16),
            pltpu.VMEM((FF, D), bf16),
            pltpu.VMEM((tab_rows, D), bf16),
            pltpu.VMEM((Z * 2 * (D // LANES), LANES), f32),
            pltpu.VMEM((E * 2 * (D // LANES), LANES), f32),
            pltpu.VMEM((8, D), f32),
            pltpu.VMEM((S, LANES), i32),
            pltpu.VMEM((S, LANES), i32),
            pltpu.VMEM((S, 2 * R), bf16),
            pltpu.VMEM((2 * R, S), bf16),
            pltpu.VMEM((R, D), f32),
            pltpu.VMEM((R, D), bf16),
            pltpu.VMEM((8, D), f32),
            pltpu.VMEM((min(128, S), D), f32),
            pltpu.VMEM((S, D), bf16),
            pltpu.VMEM((D, S), bf16),
            pltpu.VMEM((S, FF), f32),
            pltpu.VMEM((S, FF), f32),
            pltpu.VMEM((S, FF), f32),
            pltpu.VMEM((S, FF), bf16),
            pltpu.VMEM((FF, S), bf16),
            pltpu.VMEM((2, S, FF), bf16),
            pltpu.VMEM((E, D), f32),
            pltpu.VMEM((E, E, D // E), f32),
            pltpu.VMEM((2 * Z, E, D // E), f32),
            pltpu.VMEM((E, E, D // E), f32),
            pltpu.VMEM((2, Z * LANES, FF), bf16),
            pltpu.VMEM((2, Z * LANES, FF), bf16),
            pltpu.VMEM((2, Z * LANES, FF), bf16),
            pltpu.VMEM((Z, FF, LANES), bf16),
            pltpu.VMEM((Z, FF, LANES), bf16),
            pltpu.VMEM((Z, FF, LANES), bf16),
            pltpu.VMEM((2, 2, H, LANES, FF), bf16),
            pltpu.VMEM((2, 2, H, FF // 2, LANES), bf16),
            dma((4,)), dma((4,)), dma((8,)), dma((8,)),
            dma((4, 2, H)), dma((4, 2, H)), dma((4, Z)), dma((4, Z)),
            dma((2, Z)), dma((2, Z)), dma((2, Z)), dma((2, Z)), dma((Z,)), dma((Z,)),
            dma((4, 2, H)), dma((4, 2, H)),
        ],
        compiler_params=pltpu.CompilerParams(
            collective_id=0, has_side_effects=True, vmem_limit_bytes=sizes["vmem"]
        ),
        cost_estimate=pl.CostEstimate(
            flops=7 * 2 * S * D * FF, bytes_accessed=2 * 4 * S * D, transcendentals=0
        ),
    )(
        history, lengths, user_query, pos_item, lane_ints, col_ints, w_router.T,
        w_gate, w_up, w_down, out_gain.reshape(1, D),
    )
    losses, grad_gate, grad_up, grad_down, grad_router = outs
    return losses[:2, 0], grad_gate[None], grad_up[None], grad_down[None], grad_router.T


def solution(mesh):
    both = ("dp", "expert")
    n_dp, n_expert = mesh.shape["dp"], mesh.shape["expert"]

    def whole(history, lengths, user_query, pos_item, neg_index, routes, w_router, w_gate, w_up, w_down, out_gain):
        rows = routes.shape[0] // (n_dp * n_expert)
        sizes = {
            "Z": n_dp // 2, "E": n_expert, "D": history.shape[2], "FF": w_gate.shape[2],
            "CAP": min(rows, 4 * rows // n_expert), "R": rows, "vmem": 63 << 20,
        }
        return jax.shard_map(
            functools.partial(local, sizes),
            mesh=mesh,
            in_specs=(
                P(both, None, None), P(both), P(both, None), P(both, None), P(both, None),
                P(both, None), P(), P("expert", "dp", None), P("expert", "dp", None),
                P("expert", None, "dp"), P(),
            ),
            out_specs=(
                P(both), P("expert", "dp", None), P("expert", "dp", None),
                P("expert", None, "dp"), P(),
            ),
            check_vma=False,
        )(history, lengths, user_query, pos_item, neg_index, routes, w_router, w_gate, w_up, w_down, out_gain)

    return whole
```

time: 590 us -> 171 us (0.29); the launches traced: 580 us -> 170 us
  waiting for transfers between devices: 386 us -> 0 us
  Pallas kernels: 0 us -> 158 us
  local copies, waits for them, and re-layouts: 59.2 us -> 9.08 us
  matrix products: 36.6 us -> 0 us
  other arithmetic: 31.9 us -> 2.71 us
  starting transfers between devices: 26.9 us -> 0 us
  blocking collectives: 24 us -> 0 us
  between operations: 15.2 us -> 0.66 us
    psum x4 -> x0, waiting for transfers between devices: 168 us -> none  [over_axes_2(): x = lax.psum(x, axis)]
    pallas_call x0 -> x1, Pallas kernels: none -> 158 us  [local(): pl.pallas_call(functools.partial(kernel, sizes), out_shape=(jax.ShapeDtyp...]
    all_gather x3 -> x0, waiting for transfers between devices: 118 us -> none  [the longest x1 43 us: whole_of(): result = lax.all_gather(result, axes[number], axis=dim, tiled=True)]
    unnamed x9 -> x0, waiting for transfers between devices: 75.7 us -> none
    dot_general x12 -> x0, matrix products: 36.6 us -> none  [the longest x1 5.67 us: local(): jnp.einsum('uhd,uthd->uht', query_heads, key_heads, preferred_element_typ...]
    all_to_all x4 -> x0, starting transfers between devices: 26.6 us -> none  [the longest x1 8.43 us: local(): lax.all_to_all(grad_send.reshape(experts, capacity, model_width), EXPERT,...]
    all_to_all x4 -> x0, waiting for transfers between devices: 24.3 us -> none  [the longest x1 18.1 us: local(): lax.all_to_all(expert_out.reshape(expert_devs, capacity, model_width), EX...]
    all_gather x2 -> x0, blocking collectives: 24 us -> none  [the longest x1 19.5 us: local(): group_ctx = lax.all_gather(context, EXPERT, axis=0, tiled=True)]
  transfers between devices with their start and end apart: 12 -> 0, of which waited for: 10 -> 0; matrix products, arithmetic and copies ran while one was open for 15% -> 0% of each run, Pallas kernels for 0% -> 0%
where the time goes in v1:
time: 171 us; the launch traced here: 170 us
  Pallas kernels  158 us (92%)
  local copies, waits for them, and re-layouts  9.08 us (5%)
  other arithmetic  2.71 us (2%)
    pallas_call x1, Pallas kernels, local(): pl.pallas_call(functools.partial(kernel, sizes), out_shape=(jax.ShapeDtyp...  158 us
    unnamed x4, local copies, waits for them, and re-layouts  6.86 us

profile of v1, /device:TPU:1, one launch (start us, length us, event | category | flops | bytes accessed | tf_op | source)
XLA Modules:
  0.0 170.3 jit_solution(18152869904237059383)
XLA Ops:
  0.6 0.8 pad_add_fusion.2
  1.4 0.1 broadcast_in_dim_reshape.7
  1.5 0.1 broadcast_in_dim_reshape.6
  1.6 1.3 pad_add_fusion.lane_ints
  2.8 0.7 pad_add_fusion.1
  3.5 0.7 copy.20.col_ints
  4.3 157.9 %shard_map.146 = (f32[8,128]{1,0:T(8,128)}, f32[128,768]{1,0:T(8,128)}, f32[128,768]{1,0:T(8,128)}, f32[768,128]{1,0:T(8,128)}, f32[16,2048]{1,0:T(8,128)}) custom-call(bf16[2,1024,2048]{2,1,0:T(8,128)(2,1)} %hist.1, s32[2]{0:T(128)} %lens.1, bf16[2,2048]{1,0:T(2,128)(2,1)} %q_ref.1, bf16[2,2048]{1,0:T(2,128)(2,1)} %pos_ref.1, ...), custom_call_target="tpu_custom_call" | custom-call | flops 11274289152 | bytes 8388608 | tf_op jit(solution)/shard_map/pallas_call | solution.py:640
  162.2 1.3 slice_reduce_fusion
  163.5 1.8 %copy.25 = f32[1,128,768]{2,1,0:T(8,128)} copy(f32[1,128,768]{2,1,0:T(8,128)} %bitcast.9) | data formatting | bytes 786432
  165.2 1.8 %copy.26 = f32[1,128,768]{2,1,0:T(8,128)} copy(f32[1,128,768]{2,1,0:T(8,128)} %bitcast.8) | data formatting | bytes 786432
  167.0 1.8 %copy.27 = f32[1,768,128]{2,1,0:T(8,128)} copy(f32[1,768,128]{2,1,0:T(8,128)} %bitcast.7) | data formatting | bytes 786432
  168.8 1.6 copy.28
  (1 shorter events, 0.0 us)

commit v2 on v1

--- a/solution.py
+++ b/solution.py
@@ -29,9 +29,9 @@
 
 def kernel(
     sizes,
-    hist, lens, q_ref, pos_ref, lane_ints, col_ints, wr_ref, wg, wu, wd, gain_ref,
+    hist, lens, q_ref, pos_ref, neg_ref, routes_ref, wr_ref, wg, wu, wd, gain_ref,
     loss_out, gg_out, gu_out, gd_out, gr_out,
-    bufs, w_g, w_u, w_d, tab, pieces, ctx_pieces, ctx2, codes_out, codes,
+    bufs, w_g, w_u, w_d, tab, pieces, ctx_pieces, ctx2, codes,
     s01, st, xh, nloc, gq_ref, xbuf, rows, rows_t, acc_g, acc_u, acc_h,
     hid, hid_t, d_gu, r_part, r_got, r_mid, r_fin,
     g_own, g_out, g_sib, d_own, d_out, d_sib, g_ring, d_ring,
@@ -90,9 +90,6 @@
         pltpu.make_async_copy(hist.at[n // 2, pl.ds((n % 2) * S, S), :], bufs.at[n], hist_sem.at[n])
         for n in range(4)
     ]
-    for cp in hist_copies:
-        cp.start()
-
     own = (wg.at[0], wu.at[0], wd.at[0, pl.ds(0, FH), :], wd.at[0, pl.ds(FH, FH), :])
 
     def wref(t, of):
@@ -166,6 +163,20 @@
         for t in types:
             took(wref(t, 2 * at_z(off) + 1 - c), sib_r.at[t, off % Z])
 
+    LAST = Z // 2
+    events = [(t, k) for k in range(1, LAST + 1) for t in range(2)]
+
+    def advance(until=None):
+        while events:
+            if until is not None and events[0][1] > until:
+                return
+            t, k = events.pop(0)
+            ring_event((t,), k)
+            if (t, k) == (1, LAST - 1):
+                ring_begin((2, 3))
+            if until is None:
+                return
+
     my_piece = pieces.at[pl.ds(mo(z * PR, PR), PR), :]
 
     @pl.loop(1, Z)
@@ -177,9 +188,25 @@
 
     drains.append(lambda: took(pieces.at[pl.ds(0, (Z - 1) * PR), :], small_s.at[0]))
     ring_begin((0, 1))
-
-    rt0, rt1 = lane_ints[0:1, :], lane_ints[1:2, :]
-    id_lane = lane_ints[2:3, :]
+    for cp in hist_copies:
+        cp.start()
+
+    rt0, rt1 = routes_ref[0:1, :], routes_ref[1:2, :]
+    row = iota((R, 1), 0)
+    base = (dp * E + me) * 2
+    id_f = jnp.where(row == 0, base, jnp.where(row == CANDS, base + 1, 0)).astype(f32)
+    for u in range(2):
+        at = iota((R, CANDS - 1), 0) == iota((R, CANDS - 1), 1) + (u * CANDS + 1)
+        drawn = neg_ref[u : u + 1, :].astype(f32)
+        id_f = id_f + jnp.sum(jnp.where(at, drawn, 0.0), axis=1, keepdims=True)
+    diagonal = iota((R, R), 0) == iota((R, R), 1)
+    id_col = id_f.astype(i32)
+    id_lane = jnp.sum(jnp.where(diagonal, id_f, 0.0), axis=0, keepdims=True).astype(i32)
+
+    def as_column(v):
+        return jnp.sum(
+            jnp.where(diagonal, v.astype(f32), 0.0), axis=1, keepdims=True
+        ).astype(i32)
 
     def table_row(i):
         dev = lax.shift_right_logical(i, 1)
@@ -198,29 +225,27 @@
     in0, in1 = s_sub == slot0, s_sub == slot1
     s01[:, 0:R] = in0.astype(bf16)
     s01[:, R : 2 * R] = in1.astype(bf16)
-    user_lane = me * 2 + (iota((1, R), 1) >= CANDS).astype(i32)
-    code_lane = (table_row(id_lane) + user_lane * N_ITEMS + 1).astype(f32)
-    code = jnp.sum(jnp.where(in0 | in1, code_lane, 0.0), axis=1, keepdims=True).astype(i32) - 1
-    codes_out[...] = jnp.broadcast_to(code, (S, LANES))
     my_slots = pl.ds(mo(me * CAP, CAP), CAP)
-    codes[my_slots, :] = codes_out[my_slots, :]
-    to_peers(
-        lambda p: remote(
-            codes_out.at[pl.ds(mo(p * CAP, CAP), CAP), :], codes.at[my_slots, :],
-            small_s.at[1], small_r.at[1], dp, p,
-        )
-    )
-    drains.append(lambda: took(codes_out.at[pl.ds(0, S - CAP), :], small_s.at[1]))
-
-    r0, r1, id_col = col_ints[:, 0:1], col_ints[:, 1:2], col_ints[:, 2:3]
+    r0, r1 = as_column(rt0), as_column(rt1)
     e_lane = iota((R, E), 1)
     m0, m1 = e_lane == r0, e_lane == r1
     lower = (iota((R, R), 1) < iota((R, R), 0)).astype(bf16)
     rank = dot(lower, (m0 | m1).astype(bf16)) + (CAP * e_lane).astype(f32)
     s_lane = iota((R, S), 1)
+    user_col = me * 2 + (iota((R, 1), 0) >= CANDS).astype(i32)
+    code_col = (table_row(id_col) + user_col * N_ITEMS + 1).astype(f32)
+    code_row = jnp.full((1, S), -1.0, f32)
     for k, m in enumerate((m0, m1)):
         slot = jnp.sum(jnp.where(m, rank, 0.0), axis=1, keepdims=True).astype(i32)
-        st[k * R : (k + 1) * R, :] = (s_lane == slot).astype(bf16)
+        here = s_lane == slot
+        st[k * R : (k + 1) * R, :] = here.astype(bf16)
+        code_row = code_row + jnp.sum(jnp.where(here, code_col, 0.0), axis=0, keepdims=True)
+    for n in range(S // LANES):
+        codes[pl.ds(me * 8 + n, 1), :] = code_row[:, n * LANES : (n + 1) * LANES].astype(i32)
+    my_codes = codes.at[pl.ds(mo(me * 8, 8), 8), :]
+    all_codes = codes.at[pl.ds(0, (E - 1) * 8), :]
+    to_peers(lambda p: remote(my_codes, my_codes, small_s.at[1], small_r.at[1], dp, p))
+    drains.append(lambda: took(all_codes, small_s.at[1]))
 
     took(pieces.at[pl.ds(0, (Z - 1) * PR), :], small_r.at[0])
     my_block = pl.ds(mo(c * HALF + me * BLK, BLK), BLK)
@@ -258,46 +283,16 @@
         for j in range(NP):
             ctx_pieces[pl.ds(me * PR + NP * u + j, 1), :] = ctx[:, j * PC : (j + 1) * PC]
 
+    advance()
     attend(0)
-    ring_event((0, 1), 1)
     attend(1)
     my_ctx = ctx_pieces.at[pl.ds(mo(me * PR, PR), PR), :]
     to_peers(lambda p: remote(my_ctx, my_ctx, small_s.at[3], small_r.at[3], dp, p))
     drains.append(lambda: took(ctx_pieces.at[pl.ds(0, (E - 1) * PR), :], small_s.at[3]))
-
-    took(tab.at[pl.ds(0, (E - 1) * BLK), :], small_r.at[2])
-    my_half = tab.at[pl.ds(mo(c * HALF, HALF), HALF), :]
-    half_copy = remote(my_half, my_half, small_s.at[4], small_r.at[4], sib_dp, me)
-    half_copy.start()
-    drains.append(half_copy.wait_send)
     for u in range(2):
         gq_ref[u : u + 1, :] = q_ref[u : u + 1, :].astype(f32) * gain_ref[...]
-    ring_event((0, 1), 2)
-    took(my_half, small_r.at[4])
-
-    first_user = iota((R, 1), 0) < CANDS
-
-    def by_user(ref, cols):
-        return jnp.where(first_user, ref[0:1, cols], ref[1:2, cols])
-
-    oh = (iota((R, N_ITEMS), 1) == table_row(id_col)).astype(bf16)
-    NC = min(512, D)
-    total = jnp.zeros((R, 1), f32)
-    for n in range(D // NC):
-        cols = slice(n * NC, (n + 1) * NC)
-        x = dot(oh, tab[0:N_ITEMS, cols]) + by_user(ctx2, cols)
-        xh[:, cols] = x
-        total = total + jnp.sum(x * x, axis=1, keepdims=True)
-    inv = lax.rsqrt(total * (1.0 / D) + EPS)
-    for n in range(D // NC):
-        cols = slice(n * NC, (n + 1) * NC)
-        nloc[:, cols] = (xh[:, cols] * inv).astype(bf16)
-    logits = lax.dot_general(nloc[...], wr_ref[...], NT, preferred_element_type=f32)
-    affinity = jax.nn.sigmoid(logits)
-    aff0 = jnp.sum(jnp.where(m0, affinity, 0.0), axis=1, keepdims=True)
-    aff1 = jnp.sum(jnp.where(m1, affinity, 0.0), axis=1, keepdims=True)
-    aff_total = aff0 + aff1
-    mix0, mix1 = aff0 / aff_total, aff1 / aff_total
+    for _ in range(3):
+        advance()
 
     took(ctx_pieces.at[pl.ds(0, (E - 1) * PR), :], small_r.at[3])
     NU = 2 * E
@@ -309,14 +304,30 @@
             tab[N_ITEMS + n * NU : N_ITEMS + (n + 1) * NU, cols] = part
             v = v - part.astype(f32)
     tab[N_ITEMS + 3 * NU :, :] = jnp.zeros((TABW - N_ITEMS - 3 * NU, D), bf16)
-    took(codes.at[pl.ds(0, S - CAP), :], small_r.at[1])
-    ring_event((0, 1), 3) if Z > 6 else None
+    took(all_codes, small_r.at[1])
+
+    took(tab.at[pl.ds(0, (E - 1) * BLK), :], small_r.at[2])
+    my_half = tab.at[pl.ds(mo(c * HALF, HALF), HALF), :]
+    half_copy = remote(my_half, my_half, small_s.at[4], small_r.at[4], sib_dp, me)
+    half_copy.start()
+    drains.append(half_copy.wait_send)
+    advance()
+    took(my_half, small_r.at[4])
+    advance()
+
+    NC = min(512, D)
     MT = min(128, S)
 
-    @pl.loop(0, S // MT)
-    def _(m):
+    def rebuild(m):
         here = pl.ds(mo(m * MT, MT), MT)
-        got = codes[here, :]
+        PER = MT // CAP
+        shift = lax.rem(me * CAP, LANES) if CAP < LANES else 0
+        place = iota((CAP, LANES), 1) == iota((CAP, LANES), 0) + shift
+        columns = []
+        for n in range(PER):
+            line = codes[pl.ds((m * PER + n) * 8 + lax.div(me * CAP, LANES), 1), :].astype(f32)
+            columns.append(jnp.sum(jnp.where(place, line, 0.0), axis=1, keepdims=True))
+        got = jnp.broadcast_to(jnp.concatenate(columns, axis=0).astype(i32), (MT, LANES))
         item = jnp.where(got >= 0, got & (N_ITEMS - 1), -1)
         user = lax.shift_right_arithmetic(got, N_ITEMS.bit_length() - 1)
         lane = iota((MT, LANES), 1)
@@ -338,9 +349,7 @@
             rows[here, cols] = y
             rows_t[cols, here] = y.T
 
-    for k in range(3, Z // 2 + 1) if Z <= 6 else range(4, Z // 2 + 1):
-        ring_event((0, 1), k)
-    ring_begin((2, 3))
+    pl.loop(0, S // MT)(rebuild)
 
     near_first = [0]
     for k in range(1, Z // 2):
@@ -348,20 +357,26 @@
     near_first.append(Z // 2)
     FT = 256
 
-    for off in near_first:
-        if off == 0:
-            own_copies[0].wait()
-            own_copies[1].wait()
-        sib_wait((0, 1), off)
-        cols = pl.ds(mo(at_z(off) * CH, CH), CH)
-
+    def offs_at(k):
+        if k == 0 or k == LAST:
+            return [k]
+        return [k, -k]
+
+    own_copies[0].wait()
+    own_copies[1].wait()
+    for k in range(LAST + 1):
+        advance(k)
+        for off in offs_at(k):
+            sib_wait((0, 1), off)
+        parts = [pl.ds(mo(at_z(off) * CH, CH), CH) for off in offs_at(k)]
         @pl.loop(0, FF // FT)
         def _(n):
             f = pl.ds(mo(n * FT, FT), FT)
-            left = rows[:, cols]
             for acc, w in ((acc_g, w_g), (acc_u, w_u)):
-                v = dot(left, w[cols, f])
-                if off == 0:
+                v = dot(rows[:, parts[0]], w[parts[0], f])
+                for cols in parts[1:]:
+                    v = v + dot(rows[:, cols], w[cols, f])
+                if k == 0:
                     acc[:, f] = v
                 else:
                     acc[:, f] += v
@@ -402,6 +417,29 @@
     for n in range(FF // LANES):
         f = slice(n * LANES, (n + 1) * LANES)
         hid_t[f, :] = hid[:, f].T
+
+    first_user = iota((R, 1), 0) < CANDS
+
+    def by_user(ref, cols):
+        return jnp.where(first_user, ref[0:1, cols], ref[1:2, cols])
+
+    oh = (iota((R, N_ITEMS), 1) == table_row(id_col)).astype(bf16)
+    total = jnp.zeros((R, 1), f32)
+    for n in range(D // NC):
+        cols = slice(n * NC, (n + 1) * NC)
+        x = dot(oh, tab[0:N_ITEMS, cols]) + by_user(ctx2, cols)
+        xh[:, cols] = x
+        total = total + jnp.sum(x * x, axis=1, keepdims=True)
+    inv = lax.rsqrt(total * (1.0 / D) + EPS)
+    for n in range(D // NC):
+        cols = slice(n * NC, (n + 1) * NC)
+        nloc[:, cols] = (xh[:, cols] * inv).astype(bf16)
+    logits = lax.dot_general(nloc[...], wr_ref[...], NT, preferred_element_type=f32)
+    affinity = jax.nn.sigmoid(logits)
+    aff0 = jnp.sum(jnp.where(m0, affinity, 0.0), axis=1, keepdims=True)
+    aff1 = jnp.sum(jnp.where(m1, affinity, 0.0), axis=1, keepdims=True)
+    aff_total = aff0 + aff1
+    mix0, mix1 = aff0 / aff_total, aff1 / aff_total
 
     sums = [jnp.zeros((R, 1), f32) for _ in range(6)]
     for i, off in enumerate(near_first):
@@ -500,11 +538,15 @@
         cp.start()
         drains.append(cp.wait_send)
 
-    def sum_step(types, k):
-        for t in types:
-            for d in range(2):
-                if k <= HOPS[t][d]:
-                    sum_send(t, d, k)
+    def stage(types, n):
+        first, second = types
+        if n % 2:
+            first, second = second, first
+        k = LAST - (n + 1) // 2
+        for t, d in ((first, 0), (second, 1)):
+            sum_send(t, d, k)
+
+    STAGES = 2 * LAST - 1
 
     def sum_last(t, out):
         extra = []
@@ -522,10 +564,25 @@
         for t in range(2):
             took(block(theirs, t, at_z(off)), gsib_r.at[t, off % Z])
 
-    def offs_at(k):
-        if k == 0 or k == Z // 2:
-            return [k]
-        return [k, -k]
+    def down_block(off):
+        of = at_z(off)
+        g = dot(hid_t[...], bufs[3, :, pl.ds(mo(of * CH, CH), CH)])
+        low, high = g[:, :LANES], g[:, LANES:]
+        d_out[of] = jnp.where(c == 0, high, low).astype(bf16)
+        cp = remote(
+            d_out.at[of], d_sib.at[of], dsib_s.at[off % Z], dsib_r.at[off % Z], sib_dp, me
+        )
+        cp.start()
+        drains.append(cp.wait_send)
+        d_own[of] = jnp.where(c == 0, low, high).astype(bf16)
+
+    def down_pass(off):
+        down_wait(off)
+        k = abs(off)
+        for t in (3, 2):
+            for d in range(2):
+                if k == LAST and HOPS[t][d] == LAST or k < LAST and d == (off < 0):
+                    sum_send(t, d, k)
 
     i = 0
     for k in range(Z // 2, -1, -1):
@@ -539,18 +596,11 @@
                 acc_h[...] = v
             else:
                 acc_h[...] += v
-            g = dot(hid_t[...], got)
-            low, high = g[:, :LANES], g[:, LANES:]
-            d_own[of] = jnp.where(c == 0, low, high).astype(bf16)
-            d_out[of] = jnp.where(c == 0, high, low).astype(bf16)
-            cp = remote(d_out.at[of], d_sib.at[of], dsib_s.at[off % Z], dsib_r.at[off % Z], sib_dp, me)
-            cp.start()
-            drains.append(cp.wait_send)
+            if k > 0:
+                down_block(off)
+            if i > 0:
+                down_pass(far_first[i - 1])
             i += 1
-        if k + 1 <= Z // 2:
-            for off in offs_at(k + 1):
-                down_wait(off)
-            sum_step((2, 3), k + 1)
 
     @pl.loop(0, S // 64)
     def _(m):
@@ -559,6 +609,33 @@
         d_gu[0, here, :] = (dh * acc_g[here, :]).astype(bf16)
         d_gu[1, here, :] = (dh * acc_u[here, :]).astype(bf16)
 
+    def gate_block(off):
+        of = at_z(off)
+        for core, dest in ((1 - c, g_out), (c, g_own)):
+            at = pl.ds(mo((2 * of + core) * LANES, LANES), LANES)
+            to = pl.ds(mo(of * LANES, LANES), LANES)
+            for t in range(2):
+                dest[t, to, :] = dot(rows_t[at, :], d_gu[t]).astype(bf16)
+                if dest is g_out:
+                    cp = remote(
+                        block((g_out, d_out), t, of), block(theirs, t, of),
+                        gsib_s.at[t, off % Z], gsib_r.at[t, off % Z], sib_dp, me,
+                    )
+                    cp.start()
+                    drains.append(cp.wait_send)
+
+    gate_block(LAST)
+    gate_block(LAST - 1)
+    gate_wait(LAST)
+    stage((0, 1), 0)
+    if LAST > 1:
+        gate_block(1 - LAST)
+    for off in offs_at(LAST - 1):
+        gate_wait(off)
+    if STAGES > 1:
+        stage((0, 1), 1)
+    down_block(0)
+
     took(r_got.at[pl.ds(0, E - 1)], small_r.at[5])
     part = r_got[0]
     for n in range(1, E):
@@ -574,26 +651,15 @@
 
     drains.append(lambda: took(r_mid.at[pl.ds(0, 2 * Z - 1)], small_s.at[6]))
 
-    for k in range(Z // 2, -1, -1):
-        for off in reversed(offs_at(k)):
-            of = at_z(off)
-            for core, dest in ((c, g_own), (1 - c, g_out)):
-                at = pl.ds(mo((2 * of + core) * LANES, LANES), LANES)
-                to = pl.ds(mo(of * LANES, LANES), LANES)
-                left = rows_t[at, :]
-                for t in range(2):
-                    dest[t, to, :] = dot(left, d_gu[t]).astype(bf16)
-            for t in range(2):
-                cp = remote(
-                    block((g_out, d_out), t, of), block(theirs, t, of),
-                    gsib_s.at[t, off % Z], gsib_r.at[t, off % Z], sib_dp, me,
-                )
-                cp.start()
-                drains.append(cp.wait_send)
-        if k + 1 <= Z // 2:
-            for off in offs_at(k + 1):
-                gate_wait(off)
-            sum_step((0, 1), k + 1)
+    for k in range(LAST - 2, -1, -1):
+        for off in offs_at(k):
+            gate_block(off)
+        for n in (2 * (LAST - k) - 2, 2 * (LAST - k) - 1):
+            if n == 2 * (LAST - k) - 1:
+                for off in offs_at(k):
+                    gate_wait(off)
+            if n < STAGES:
+                stage((0, 1), n)
 
     down_wait(0)
     sum_last(2, gd_out.at[pl.ds(0, FH), :])
@@ -612,11 +678,19 @@
     for n in range(E):
         gr_out[:, n * DB : (n + 1) * DB] = r_fin[n]
 
-    gate_wait(0)
     sum_last(0, gg_out)
     sum_last(1, gu_out)
     for drain in drains:
         drain()
+
+
+def hand_out(loss, gg, gu, gd, gr, loss_out, gg_out, gu_out, gd_out, gr_out):
+    gg_out[0] = gg[...]
+    gu_out[0] = gu[...]
+    gd_out[0] = gd[...]
+    gr_out[...] = gr[...]
+    for u in range(2):
+        loss_out[u] = loss[u, 0]
 
 
 def local(
@@ -625,18 +699,13 @@
 ):
     Z, E, D, FF, CAP, R = (sizes[k] for k in ("Z", "E", "D", "FF", "CAP", "R"))
     S = E * CAP
-    base = (lax.axis_index("dp") * E + lax.axis_index("expert")) * 2
-    ids = jnp.concatenate(
-        [base + jnp.arange(2, dtype=i32)[:, None], neg_index], axis=1
-    ).reshape(R)
-    lane_ints = jnp.concatenate([routes.T, ids[None, :]], axis=0)
-    col_ints = jnp.concatenate([routes, ids[:, None]], axis=1)
     n_items = 4 * Z * E
     tab_rows = n_items + LANES
     H = max(Z // 2, 1)
     dma = pltpu.SemaphoreType.DMA
     vmem = pl.BlockSpec(memory_space=pltpu.VMEM)
     hbm = pl.BlockSpec(memory_space=pl.ANY)
+    smem = pl.BlockSpec(memory_space=pltpu.SMEM)
     outs = pl.pallas_call(
         functools.partial(kernel, sizes),
         out_shape=(
@@ -647,7 +716,7 @@
             jax.ShapeDtypeStruct((E, D), f32),
         ),
         in_specs=[
-            hbm, pl.BlockSpec(memory_space=pltpu.SMEM), vmem, vmem, vmem, vmem, vmem,
+            hbm, smem, vmem, vmem, vmem, vmem, vmem,
             hbm, hbm, hbm, vmem,
         ],
         out_specs=(vmem,) * 5,
@@ -660,8 +729,7 @@
             pltpu.VMEM((Z * 2 * (D // LANES), LANES), f32),
             pltpu.VMEM((E * 2 * (D // LANES), LANES), f32),
             pltpu.VMEM((8, D), f32),
-            pltpu.VMEM((S, LANES), i32),
-            pltpu.VMEM((S, LANES), i32),
+            pltpu.VMEM((E * 8, LANES), i32),
             pltpu.VMEM((S, 2 * R), bf16),
             pltpu.VMEM((2 * R, S), bf16),
             pltpu.VMEM((R, D), f32),
@@ -700,11 +768,22 @@
             flops=7 * 2 * S * D * FF, bytes_accessed=2 * 4 * S * D, transcendentals=0
         ),
     )(
-        history, lengths, user_query, pos_item, lane_ints, col_ints, w_router.T,
+        history, lengths, user_query, pos_item, neg_index, routes.T, w_router.T,
         w_gate, w_up, w_down, out_gain.reshape(1, D),
     )
-    losses, grad_gate, grad_up, grad_down, grad_router = outs
-    return losses[:2, 0], grad_gate[None], grad_up[None], grad_down[None], grad_router.T
+    losses, grad_gate, grad_up, grad_down, grad_router = pl.pallas_call(
+        hand_out,
+        out_shape=(
+            jax.ShapeDtypeStruct((2,), f32),
+            jax.ShapeDtypeStruct((1, LANES, FF), f32),
+            jax.ShapeDtypeStruct((1, LANES, FF), f32),
+            jax.ShapeDtypeStruct((1, FF, LANES), f32),
+            jax.ShapeDtypeStruct((E, D), f32),
+        ),
+        in_specs=[smem, vmem, vmem, vmem, vmem],
+        out_specs=(smem, vmem, vmem, vmem, vmem),
+    )(*outs)
+    return losses, grad_gate, grad_up, grad_down, grad_router.T
 
 
 def solution(mesh):

time: 171 us -> 154 us (0.901)
  local copies, waits for them, and re-layouts: 9.08 us -> 0 us
  Pallas kernels: 158 us -> 153 us
  other arithmetic: 2.71 us -> 0 us
    unnamed x4 -> x0, local copies, waits for them, and re-layouts: 6.86 us -> none
    pallas_call x1, Pallas kernels: 158 us -> 151 us  [local(): pl.pallas_call(functools.partial(kernel, sizes), out_shape=(jax.ShapeDtyp...]
    concatenate x3 -> x0, other arithmetic: 2.7 us -> none  [the longest x1 1.26 us: local(): lane_ints = jnp.concatenate([routes.T, ids[None, :]], axis=0)]
    pallas_call x0 -> x1, Pallas kernels: none -> 2.35 us  [local(): pl.pallas_call(hand_out, out_shape=(jax.ShapeDtypeStruct((2,), f32), jax....]
where the time goes in v2:
time: 154 us
  Pallas kernels  153 us (99%)
    pallas_call x1, Pallas kernels, local(): pl.pallas_call(functools.partial(kernel, sizes), out_shape=(jax.ShapeDtyp...  151 us

profile of v2, /device:TPU:1, one launch (start us, length us, event | category | flops | bytes accessed | tf_op | source)
XLA Modules:
  0.0 154.2 jit_solution(12753618576453573203)
XLA Ops:
  0.6 151.1 %shard_map.146 = (f32[8,128]{1,0:T(8,128)}, f32[128,768]{1,0:T(8,128)}, f32[128,768]{1,0:T(8,128)}, f32[768,128]{1,0:T(8,128)}, f32[16,2048]{1,0:T(8,128)}) custom-call(bf16[2,1024,2048]{2,1,0:T(8,128)(2,1)} %hist.1, s32[2]{0:T(128)} %lens.1, bf16[2,2048]{1,0:T(2,128)(2,1)} %q_ref.1, bf16[2,2048]{1,0:T(2,128)(2,1)} %pos_ref.1, s32[2,63]{1,0:T(2,128)} %neg_ref.1, ...), custom_call_target="tpu_custom_call" | custom-call | flops 11274289152 | bytes 8388608 | tf_op jit(solution)/shard_map/pallas_call | solution.py:709
  151.7 2.3 %shard_map.147 = (f32[2]{0:T(128)}, f32[1,128,768]{2,1,0:T(8,128)}, f32[1,128,768]{2,1,0:T(8,128)}, f32[1,768,128]{2,1,0:T(8,128)}, f32[16,2048]{1,0:T(8,128)}) custom-call(f32[8,128]{1,0:T(8,128)} %get-tuple-element.15.loss, f32[128,768]{1,0:T(8,128)} %get-tuple-element.16.gg, f32[128,768]{1,0:T(8,128)} %get-tuple-element.17.gu, ...), custom_call_target="tpu_custom_call" | custom-call | tf_op jit(solution)/shard_map/pallas_call | solution.py:774

commit v3 on v2

--- a/solution.py
+++ b/solution.py
@@ -190,6 +190,51 @@
     ring_begin((0, 1))
     for cp in hist_copies:
         cp.start()
+
+    took(pieces.at[pl.ds(0, (Z - 1) * PR), :], small_r.at[0])
+    my_block = pl.ds(mo(c * HALF + me * BLK, BLK), BLK)
+    for j in range(NP):
+        tab[my_block, j * PC : (j + 1) * PC] = pieces[pl.ds(j, BLK, stride=NP), :].astype(bf16)
+    to_peers(
+        lambda p: remote(
+            tab.at[my_block, :], tab.at[my_block, :], small_s.at[2], small_r.at[2], dp, p
+        )
+    )
+    drains.append(lambda: took(tab.at[pl.ds(0, (E - 1) * BLK), :], small_s.at[2]))
+
+    in_head = lax.shift_right_logical(iota((HEADS, D), 1), 7) == iota((HEADS, D), 0)
+
+    def attend(u):
+        hist_copies[2 * u].wait()
+        hist_copies[2 * u + 1].wait()
+        qd = jnp.where(in_head, q_ref[u : u + 1, :].astype(f32), 0.0).astype(bf16)
+        halves, tops = [], []
+        for n in range(2):
+            s = lax.dot_general(qd, bufs[2 * u + n], NT, preferred_element_type=f32)
+            s = s * (1.0 / math.sqrt(HEAD))
+            live = (iota((HEADS, S), 1) + n * S) < lens[u]
+            s = jnp.where(live, s, -1e30)
+            halves.append((s, live))
+            tops.append(jnp.max(s, axis=1, keepdims=True))
+        top = jnp.maximum(tops[0], tops[1])
+        w = [jnp.where(live, jnp.exp(s - top), 0.0) for s, live in halves]
+        total = jnp.sum(w[0], axis=1, keepdims=True) + jnp.sum(w[1], axis=1, keepdims=True)
+        pooled = dot((w[0] / total).astype(bf16), bufs[2 * u]) + dot(
+            (w[1] / total).astype(bf16), bufs[2 * u + 1]
+        )
+        ctx = jnp.sum(jnp.where(in_head, pooled, 0.0), axis=0, keepdims=True)
+        ctx2[u : u + 1, :] = ctx
+        for j in range(NP):
+            ctx_pieces[pl.ds(me * PR + NP * u + j, 1), :] = ctx[:, j * PC : (j + 1) * PC]
+
+    attend(0)
+    attend(1)
+    my_ctx = ctx_pieces.at[pl.ds(mo(me * PR, PR), PR), :]
+    to_peers(lambda p: remote(my_ctx, my_ctx, small_s.at[3], small_r.at[3], dp, p))
+    drains.append(lambda: took(ctx_pieces.at[pl.ds(0, (E - 1) * PR), :], small_s.at[3]))
+    for u in range(2):
+        gq_ref[u : u + 1, :] = q_ref[u : u + 1, :].astype(f32) * gain_ref[...]
+    advance()
 
     rt0, rt1 = routes_ref[0:1, :], routes_ref[1:2, :]
     row = iota((R, 1), 0)
@@ -247,50 +292,6 @@
     to_peers(lambda p: remote(my_codes, my_codes, small_s.at[1], small_r.at[1], dp, p))
     drains.append(lambda: took(all_codes, small_s.at[1]))
 
-    took(pieces.at[pl.ds(0, (Z - 1) * PR), :], small_r.at[0])
-    my_block = pl.ds(mo(c * HALF + me * BLK, BLK), BLK)
-    for j in range(NP):
-        tab[my_block, j * PC : (j + 1) * PC] = pieces[pl.ds(j, BLK, stride=NP), :].astype(bf16)
-    to_peers(
-        lambda p: remote(
-            tab.at[my_block, :], tab.at[my_block, :], small_s.at[2], small_r.at[2], dp, p
-        )
-    )
-    drains.append(lambda: took(tab.at[pl.ds(0, (E - 1) * BLK), :], small_s.at[2]))
-
-    in_head = lax.shift_right_logical(iota((HEADS, D), 1), 7) == iota((HEADS, D), 0)
-
-    def attend(u):
-        hist_copies[2 * u].wait()
-        hist_copies[2 * u + 1].wait()
-        qd = jnp.where(in_head, q_ref[u : u + 1, :].astype(f32), 0.0).astype(bf16)
-        halves, tops = [], []
-        for n in range(2):
-            s = lax.dot_general(qd, bufs[2 * u + n], NT, preferred_element_type=f32)
-            s = s * (1.0 / math.sqrt(HEAD))
-            live = (iota((HEADS, S), 1) + n * S) < lens[u]
-            s = jnp.where(live, s, -1e30)
-            halves.append((s, live))
-            tops.append(jnp.max(s, axis=1, keepdims=True))
-        top = jnp.maximum(tops[0], tops[1])
-        w = [jnp.where(live, jnp.exp(s - top), 0.0) for s, live in halves]
-        total = jnp.sum(w[0], axis=1, keepdims=True) + jnp.sum(w[1], axis=1, keepdims=True)
-        pooled = dot((w[0] / total).astype(bf16), bufs[2 * u]) + dot(
-            (w[1] / total).astype(bf16), bufs[2 * u + 1]
-        )
-        ctx = jnp.sum(jnp.where(in_head, pooled, 0.0), axis=0, keepdims=True)
-        ctx2[u : u + 1, :] = ctx
-        for j in range(NP):
-            ctx_pieces[pl.ds(me * PR + NP * u + j, 1), :] = ctx[:, j * PC : (j + 1) * PC]
-
-    advance()
-    attend(0)
-    attend(1)
-    my_ctx = ctx_pieces.at[pl.ds(mo(me * PR, PR), PR), :]
-    to_peers(lambda p: remote(my_ctx, my_ctx, small_s.at[3], small_r.at[3], dp, p))
-    drains.append(lambda: took(ctx_pieces.at[pl.ds(0, (E - 1) * PR), :], small_s.at[3]))
-    for u in range(2):
-        gq_ref[u : u + 1, :] = q_ref[u : u + 1, :].astype(f32) * gain_ref[...]
     for _ in range(3):
         advance()
 

time: 154 us -> 154 us (level)
  no operation moved by 1% of the time
where the time goes in v3:
time: 154 us
  Pallas kernels  153 us (99%)
    pallas_call x1, Pallas kernels, local(): pl.pallas_call(functools.partial(kernel, sizes), out_shape=(jax.ShapeDtyp...  151 us

profile of v3, /device:TPU:1, one launch (start us, length us, event | category | flops | bytes accessed | tf_op | source)
XLA Modules:
  0.0 153.8 jit_solution(8703265783692825387)
XLA Ops:
  0.6 150.7 %shard_map.146 = (f32[8,128]{1,0:T(8,128)}, f32[128,768]{1,0:T(8,128)}, f32[128,768]{1,0:T(8,128)}, f32[768,128]{1,0:T(8,128)}, f32[16,2048]{1,0:T(8,128)}) custom-call(bf16[2,1024,2048]{2,1,0:T(8,128)(2,1)} %hist.1, s32[2]{0:T(128)} %lens.1, bf16[2,2048]{1,0:T(2,128)(2,1)} %q_ref.1, bf16[2,2048]{1,0:T(2,128)(2,1)} %pos_ref.1, s32[2,63]{1,0:T(2,128)} %neg_ref.1, ...), custom_call_target="tpu_custom_call" | custom-call | flops 11274289152 | bytes 8388608 | tf_op jit(solution)/shard_map/pallas_call | solution.py:710
  151.3 2.3 %shard_map.147 = (f32[2]{0:T(128)}, f32[1,128,768]{2,1,0:T(8,128)}, f32[1,128,768]{2,1,0:T(8,128)}, f32[1,768,128]{2,1,0:T(8,128)}, f32[16,2048]{1,0:T(8,128)}) custom-call(f32[8,128]{1,0:T(8,128)} %get-tuple-element.15.loss, f32[128,768]{1,0:T(8,128)} %get-tuple-element.16.gg, f32[128,768]{1,0:T(8,128)} %get-tuple-element.17.gu, ...), custom_call_target="tpu_custom_call" | custom-call | tf_op jit(solution)/shard_map/pallas_call | solution.py:775
